TPU v7x, 256 devices: a whole 4x4x8 slice. The times are simulated.
256 devices in a mesh: dp: 32 (over z, y), expert: 8 (over x, core).
Axes of the slice: x: 4, y: 4, z: 8, core: 2. Of those that a mesh axis runs over, the one named last changes fastest.
Arguments:
- grad: bfloat16 [128, 1024, 768], P('expert', 'dp'), may hold values from -1200 to 1200
- momentum: float32 [128, 1024, 768], P('expert', 'dp'), may hold values from -3 to 3
Outputs:
- new_momentum: float32 [128, 1024, 768], P('expert', 'dp')
- update: float32 [128, 1024, 768], P('expert', 'dp')
All inputs are finite; a program needn't handle non-finite values.
Results may differ from a plain program's by a relative error of at most 0.0003.
Values sent between devices are 32-bit elements; how exact they have to be, the bound alone decides.
No kernel may reach another device: no remote copies, remote signals or barrier semaphores. Data moves between devices by JAX's collectives and lax.ppermute only.
A program may use at most 64 MiB of HBM per device.

v0:
```python
import math

import jax
import jax.numpy as jnp
from jax import lax
from jax.sharding import PartitionSpec as P

R = 1024
C = 768
ITERS = 2

A0, A1, A2 = 3.4445, -4.775, 2.0315


def mm(a, b):
    return jnp.dot(a, b, precision=lax.Precision.HIGH, preferred_element_type=jnp.float32)


def gram_of(x):
    return lax.dot_general(
        x, x, (((0,), (0,)), ((), ())),
        precision=lax.Precision.HIGH, preferred_element_type=jnp.float32,
    )


def swap_cores(x):
    n = lax.axis_size("expert")
    return lax.ppermute(x, "expert", [(i, i ^ 1) for i in range(n)])


def global_sum(part):
    n = lax.axis_size("dp") * lax.axis_size("expert")
    tile = jnp.broadcast_to(part, (n, 1, 128))
    got = lax.all_to_all(tile, ("dp", "expert"), split_axis=0, concat_axis=0, tiled=True)
    return jnp.sum(got[:, 0, 0])


def poly(gram):
    eye = jnp.eye(C, dtype=jnp.float32)
    return A0 * eye + (A1 * gram + A2 * mm(gram, gram))


def body(grad, momentum):
    groups, slice_rows, columns = grad.shape
    n_rows = lax.axis_size("dp")
    core = lax.axis_index("expert") % 2
    half = slice_rows // 2
    count = groups * slice_rows * columns * n_rows * lax.axis_size("expert")
    widened = grad.astype(jnp.float32)
    total = global_sum(jnp.sum(widened * widened))
    factor = jnp.minimum(1.0, 0.5 / jnp.sqrt(total / count + 1e-06))
    clipped = widened * factor
    new_momentum = 0.95 * momentum + clipped
    advance = clipped + 0.95 * new_momentum

    keep = lax.dynamic_slice_in_dim(advance, core * half, half, 1)
    give = lax.dynamic_slice_in_dim(advance, (1 - core) * half, half, 1)
    got = swap_cores(give)
    outgoing = jnp.where(
        core == 0, jnp.concatenate([keep, got], 0), jnp.concatenate([got, keep], 0)
    )
    own = lax.all_to_all(outgoing, "dp", split_axis=0, concat_axis=0, tiled=True)
    own = own.reshape(n_rows * half, columns)
    other = swap_cores(own)

    raw = gram_of(own) + gram_of(other)
    norm = jnp.sqrt(jnp.sum(own * own) + jnp.sum(other * other)) + 1e-07
    inverse = 1.0 / norm
    gram = raw * inverse * inverse
    m0 = poly(gram)
    first = mm(own * inverse, m0)
    m1 = poly(mm(mm(gram, m0), m0))
    finished = mm(first, m1) * (0.2 * math.sqrt(max(R, C)))

    back = lax.all_to_all(
        finished.reshape(n_rows, half, columns), "dp", split_axis=0, concat_axis=0, tiled=True
    )
    mine = lax.dynamic_slice_in_dim(back, core * groups, groups, 0)
    theirs = lax.dynamic_slice_in_dim(back, (1 - core) * groups, groups, 0)
    got = swap_cores(theirs)
    update = jnp.where(
        core == 0, jnp.concatenate([mine, got], 1), jnp.concatenate([got, mine], 1)
    )
    return (new_momentum, update)


def solution(mesh):
    in_specs = (P("expert", "dp", None), P("expert", "dp", None))
    out_specs = (P("expert", "dp", None), P("expert", "dp", None))
    return jax.shard_map(body, mesh=mesh, in_specs=in_specs, out_specs=out_specs, check_vma=False)
```

profile of v0, /device:TPU:1, one launch (start us, length us, event | category | flops | bytes accessed | tf_op | source)
XLA Modules:
  0.0 162.0 jit_solution(16707237567139559807)
XLA Ops:
  0.6 2.1 %fusion.11 = f32[]{:T(128)} fusion(bf16[16,32,768]{2,1,0:T(8,128)(2,1)} %param.2), kind=kLoop, calls=%fused_computation.17 | loop fusion | flops 1179647 | bytes 786436 | tf_op jit(solution)/shard_map/reduce_sum | solution.py:50
  2.8 1.4 broadcast_in_dim.3
  4.1 15.7 %all-to-all-start = ((f32[256,1,128]{2,1,0:T(1,128)}), f32[256,1,128]{2,1,0:T(1,128)S(1)}, u32[]{:S(2)}, u32[]{:S(2)}) async-start(f32[256,1,128]{2,1,0:T(1,128)} %broadcast_in_dim.3), calls=%async_computation | async-start | bytes 262144 | tf_op jit(solution)/shard_map/all_to_all | solution.py:34
  19.8 12.9 %all-to-all-done = f32[256,1,128]{2,1,0:T(1,128)S(1)} async-done(((f32[256,1,128]{2,1,0:T(1,128)}), f32[256,1,128]{2,1,0:T(1,128)S(1)}, u32[]{:S(2)}, u32[]{:S(2)}) %all-to-all-start) | async-done | bytes 131104 | tf_op jit(solution)/shard_map/all_to_all | solution.py:34
  32.7 0.9 slice_reduce_fusion
  34.3 3.2 %fusion.6 = (f32[16,32,768]{2,1,0:T(8,128)S(1)}, f32[16,32,768]{2,1,0:T(8,128)}) fusion(bf16[16,32,768]{2,1,0:T(8,128)(2,1)} %param.2, f32[]{:T(128)S(6)} %min.3, f32[16,32,768]{2,1,0:T(8,128)} %param.3), kind=kLoop, calls=%fused_computation.12 | loop fusion | flops 2359296 | bytes 5505028 | tf_op jit(solution)/shard_map/add | solution.py:54
  37.6 0.6 collective-permute-start
  38.2 1.9 %collective-permute-done = f32[16,16,768]{2,1,0:T(8,128)S(1)} collective-permute-done((f32[16,16,768]{2,1,0:T(8,128)S(1)}, f32[16,16,768]{2,1,0:T(8,128)S(1)}, u32[]{:S(2)}, u32[]{:S(2)}) %collective-permute-start) | collective-permute-done | bytes 786464 | tf_op jit(solution)/shard_map/ppermute | solution.py:28
  40.2 42.2 %all_to_all.15 = f32[32,16,768]{2,1,0:T(8,128)S(1)} all-to-all(f32[32,16,768]{2,1,0:T(8,128)S(1)} %maximum_select_fusion), channel_id=1, replica_groups=mesh['dp'=32,'expert'=8] {'dp'}, dimensions={0} | all-to-all | bytes 3145728 | tf_op jit(solution)/shard_map/all_to_all | solution.py:62
  82.5 2.3 %collective-permute-start.1 = (f32[512,768]{1,0:T(8,128)S(1)}, f32[512,768]{1,0:T(8,128)S(1)}, u32[]{:S(2)}, u32[]{:S(2)}) collective-permute-start(f32[512,768]{1,0:T(8,128)S(1)} %bitcast.19), channel_id=1, source_target_pairs={{0,1},{1,0},{2,3},{3,2},{4,5},{5,4},{6,7},{7,6},{8,9},{9,8},{10,11... | collective-permute-start | bytes 4718600 | tf_op jit(solution)/shard_map/ppermute | solution.py:28
  84.8 1.0 multiply_reduce_fusion.1
  85.8 3.7 %fusion.48 = f32[768,768,1]{1,0,2:T(8,128)} fusion(f32[32,16,768]{2,1,0:T(8,128)S(1)} %all_to_all.15), kind=kOutput, calls=%fused_computation.62 | convolution fusion | flops 1811939328 | bytes 3932160 | tf_op jit(solution)/shard_map/dot_general | solution.py:20
  89.5 1.0 multiply_reduce_fusion
  91.8 4.2 %fusion.2 = f32[768,768]{1,0:T(8,128)S(1)} fusion(f32[768,768,1]{1,0,2:T(8,128)} %fusion.48, f32[512,768]{1,0:T(8,128)S(1)} %collective-permute-done.1, f32[]{:T(128)S(6)} %div.11), kind=kOutput, calls=%fused_computation.5 | convolution fusion | flops 1813708800 | bytes 6291460 | tf_op jit(solution)/shard_map/dot_general | solution.py:20
  96.0 3.1 %fusion.49 = f32[768,768]{1,0:T(8,128)S(1)} fusion(f32[768,768]{1,0:T(8,128)S(1)} %fusion.2), kind=kOutput, calls=%fused_computation.63 | convolution fusion | flops 2717908992 | bytes 4718592 | tf_op jit(solution)/shard_map/dot_general | solution.py:16
  99.1 2.3 %fusion.10 = f32[512,768]{1,0:T(8,128)S(1)} fusion(f32[768,768]{1,0:T(8,128)S(1)} %fusion.49, f32[768,768]{1,0:T(8,128)S(1)} %fusion.2, f32[512,768]{1,0:T(8,128)S(1)} %bitcast.20, f32[]{:T(128)S(6)} %div.11), kind=kOutput, calls=%fused_computation.16 | convolution fusion | flops 1815871488 | bytes 7864324 | tf_op jit(solution)/shard_map/dot_general | solution.py:16
  101.4 3.5 %fusion.9 = f32[768,768]{1,0:T(8,128)S(1)} fusion(f32[768,768]{1,0:T(8,128)S(1)} %fusion.2, f32[768,768]{1,0:T(8,128)S(1)} %fusion.49), kind=kOutput, calls=%fused_computation.15 | convolution fusion | flops 2721447936 | bytes 7077888 | tf_op jit(solution)/shard_map/dot_general | solution.py:16
  104.9 3.2 %fusion.8 = f32[768,768]{1,0:T(8,128)S(1)} fusion(f32[768,768]{1,0:T(8,128)S(1)} %fusion.9, f32[768,768]{1,0:T(8,128)S(1)} %fusion.49, f32[768,768]{1,0:T(8,128)S(1)} %fusion.2), kind=kOutput, calls=%fused_computation.14 | convolution fusion | flops 2721447936 | bytes 9437184 | tf_op jit(solution)/shard_map/dot_general | solution.py:16
  108.2 3.2 %fusion.50 = f32[768,768]{1,0:T(8,128)S(1)} fusion(f32[768,768]{1,0:T(8,128)S(1)} %fusion.8), kind=kOutput, calls=%fused_computation.64 | convolution fusion | flops 2717908992 | bytes 4718592 | tf_op jit(solution)/shard_map/dot_general | solution.py:16
  111.3 2.3 %fusion.13 = f32[512,768]{1,0:T(8,128)S(1)} fusion(f32[512,768]{1,0:T(8,128)S(1)} %fusion.10, f32[768,768]{1,0:T(8,128)S(1)} %fusion.50, f32[768,768]{1,0:T(8,128)S(1)} %fusion.8), kind=kOutput, calls=%fused_computation.23 | convolution fusion | flops 1815871488 | bytes 7864320 | tf_op jit(solution)/shard_map/dot_general | solution.py:16
  113.6 44.0 %all_to_all.16 = f32[32,16,768]{2,1,0:T(8,128)S(1)} all-to-all(f32[32,16,768]{2,1,0:T(8,128)S(1)} %bitcast.21), channel_id=1, replica_groups=mesh['dp'=32,'expert'=8] {'dp'}, dimensions={0} | all-to-all | bytes 3145728 | tf_op jit(solution)/shard_map/all_to_all | solution.py:75
  157.8 1.0 collective-permute-start.2
  158.8 1.9 %collective-permute-done.2 = f32[16,16,768]{2,1,0:T(8,128)S(1)} collective-permute-done((f32[16,16,768]{2,1,0:T(8,128)S(1)}, f32[16,16,768]{2,1,0:T(8,128)S(1)}, u32[]{:S(2)}, u32[]{:S(2)}) %collective-permute-start.2) | collective-permute-done | bytes 786464 | tf_op jit(solution)/shard_map/ppermute | solution.py:28
  160.7 1.3 maximum_select_fusion.1
  (4 shorter events, 0.4 us)
Async XLA Ops:
  4.1 28.6 %all-to-all-start = ((f32[256,1,128]{2,1,0:T(1,128)}), f32[256,1,128]{2,1,0:T(1,128)S(1)}, u32[]{:S(2)}, u32[]{:S(2)}) async-start(f32[256,1,128]{2,1,0:T(1,128)} %broadcast_in_dim.3), calls=%async_computation | async-start | bytes 262144 | tf_op jit(solution)/shard_map/all_to_all | solution.py:34
  37.6 2.5 %collective-permute-start = (f32[16,16,768]{2,1,0:T(8,128)S(1)}, f32[16,16,768]{2,1,0:T(8,128)S(1)}, u32[]{:S(2)}, u32[]{:S(2)}) collective-permute-start(f32[16,16,768]{2,1,0:T(8,128)S(1)} %get-tuple-element.11), channel_id=1, source_target_pairs={{0,1},{1,0},{2,3},{3,2},{4,5},{5,4},{6,7},{7,6},{8,9},{9,8},{10,11... | collective-permute-start | bytes 2359304 | tf_op jit(solution)/shard_map/ppermute | solution.py:28
  82.5 7.0 %collective-permute-start.1 = (f32[512,768]{1,0:T(8,128)S(1)}, f32[512,768]{1,0:T(8,128)S(1)}, u32[]{:S(2)}, u32[]{:S(2)}) collective-permute-start(f32[512,768]{1,0:T(8,128)S(1)} %bitcast.19), channel_id=1, source_target_pairs={{0,1},{1,0},{2,3},{3,2},{4,5},{5,4},{6,7},{7,6},{8,9},{9,8},{10,11... | collective-permute-start | bytes 4718600 | tf_op jit(solution)/shard_map/ppermute | solution.py:28
  157.8 2.9 %collective-permute-start.2 = (f32[16,16,768]{2,1,0:T(8,128)S(1)}, f32[16,16,768]{2,1,0:T(8,128)S(1)}, u32[]{:S(2)}, u32[]{:S(2)}) collective-permute-start(f32[16,16,768]{2,1,0:T(8,128)S(1)} %get-tuple-element.9), channel_id=1, source_target_pairs={{0,1},{1,0},{2,3},{3,2},{4,5},{5,4},{6,7},{7,6},{8,9},{9,8},{10,11... | collective-permute-start | bytes 2359304 | tf_op jit(solution)/shard_map/ppermute | solution.py:28
where the time goes:
time: 162 us
  blocking collectives  86.3 us (53%)
  matrix products  25.4 us (16%)
  starting transfers between devices  19.6 us (12%)
  waiting for transfers between devices  16.7 us (10%)
  other arithmetic  9.61 us (6%)
  between operations  2.73 us (2%)
    all_to_all x1, blocking collectives, body(): lax.all_to_all(finished.reshape(n_rows, half, columns), 'dp', split_axis=...  44 us
    all_to_all x1, blocking collectives, body(): lax.all_to_all(outgoing, 'dp', split_axis=0, concat_axis=0, tiled=True)  42.2 us
    dot_general x6, matrix products, mm(): jnp.dot(a, b, precision=lax.Precision.HIGH, preferred_element_type=jnp.fl...  17.6 us
    all_to_all x1, starting transfers between devices, global_sum(): lax.all_to_all(tile, ('dp', 'expert'), split_axis=0, concat_axis=0, tiled...  15.7 us
    all_to_all x1, waiting for transfers between devices, global_sum(): lax.all_to_all(tile, ('dp', 'expert'), split_axis=0, concat_axis=0, tiled...  12.9 us
    dot_general x2, matrix products, gram_of(): lax.dot_general(x, x, (((0,), (0,)), ((), ())), precision=lax.Precision.H...  7.87 us
    ppermute x3, starting transfers between devices, swap_cores(): return lax.ppermute(x, 'expert', [(i, i ^ 1) for i in range(n)])  3.97 us
    ppermute x3, waiting for transfers between devices, swap_cores(): return lax.ppermute(x, 'expert', [(i, i ^ 1) for i in range(n)])  3.83 us
  transfers between devices with their start and end apart: 4, of which 3 were waited for; matrix products, arithmetic and copies ran while one was open for 3% of the time, Pallas kernels for 0%

commit v1 on v0

v1 whole, which is shorter than its diff:
```python
import math

import jax
import jax.numpy as jnp
from jax import lax
from jax.experimental import pallas as pl
from jax.experimental.pallas import tpu as pltpu
from jax.sharding import PartitionSpec as P

R = 1024
C = 768
ITERS = 2
BLOCK = 256
NB = C // BLOCK
PAIRS = [(i, j) for i in range(NB) for j in range(i, NB)]

A0, A1, A2 = 3.4445, -4.775, 2.0315
F32 = jnp.float32
BF16 = jnp.bfloat16

VMEM = pl.BlockSpec(memory_space=pltpu.VMEM)
SMEM = pl.BlockSpec(memory_space=pltpu.SMEM)
HBM = pl.BlockSpec(memory_space=pl.ANY)


def params(mib):
    return pltpu.CompilerParams(vmem_limit_bytes=mib << 20)


def swap_cores(x):
    n = lax.axis_size("expert")
    return lax.ppermute(x, "expert", [(i, i ^ 1) for i in range(n)])


def split(v):
    hi = v.astype(BF16)
    return hi, (v - hi.astype(F32)).astype(BF16)


def dot(a, b):
    return jnp.dot(a, b, preferred_element_type=F32)


def dot3(ah, al, bh, bl):
    return dot(ah, bh) + (dot(ah, bl) + dot(al, bh))


def blk(i):
    return pl.ds(i * BLOCK, BLOCK)


def put_symmetric(h, l, i, j, v):
    h[blk(i), blk(j)], l[blk(i), blk(j)] = split(v)
    if i != j:
        h[blk(j), blk(i)], l[blk(j), blk(i)] = split(v.T)


def split_both_ways(x_ref, xh, xl, th, tl):
    for j in range(NB):
        v = x_ref[:, blk(j)]
        xh[:, blk(j)], xl[:, blk(j)] = split(v)
        th[blk(j), :], tl[blk(j), :] = split(v.T)


def prepare_kernel(core_ref, grad_ref, momentum_ref, sum_ref, give_ref):
    half = grad_ref.shape[1] // 2
    rows = pl.ds(pl.multiple_of((1 - core_ref[0]) * half, half), half)
    total = jnp.zeros(grad_ref.shape[1:], F32)
    for i in range(grad_ref.shape[0]):
        v = grad_ref[i].astype(F32)
        total = total + v * v
        give_ref[0, i] = grad_ref[i, rows, :].astype(F32)
        give_ref[1, i] = momentum_ref[i, rows, :]
    total = jnp.sum(jnp.sum(total, axis=0, keepdims=True), axis=1, keepdims=True)
    sum_ref[...] = jnp.broadcast_to(total[None], sum_ref.shape)


def momentum_kernel(factor_ref, grad_ref, momentum_ref, out_ref):
    factor = factor_ref[:1, :1]
    for i in range(grad_ref.shape[0]):
        out_ref[i] = 0.95 * momentum_ref[i] + grad_ref[i].astype(F32) * factor


def place_kernel(of_core, core_ref, values_ref, *refs):
    out_ref, sem = refs[-2:]
    groups, slice_rows, _ = out_ref.shape
    half = slice_rows // 2
    core = core_ref[0] if of_core else 1 - core_ref[0]
    source = values_ref.at[pl.ds(core * groups, groups)] if of_core else values_ref
    rows = pl.ds(pl.multiple_of(core * half, half), half)
    copy = pltpu.make_async_copy(source, out_ref.at[:, rows, :], sem)
    copy.start()
    copy.wait()


def place(of_core, core, values, shape, before=()):
    return pl.pallas_call(
        lambda *refs: place_kernel(of_core, *refs),
        out_shape=jax.ShapeDtypeStruct(shape, F32),
        in_specs=[SMEM, HBM] + [HBM] * len(before),
        out_specs=HBM,
        scratch_shapes=[pltpu.SemaphoreType.DMA],
        input_output_aliases={2: 0} if before else {},
        compiler_params=params(1),
        name="place",
    )(core, values, *before)


def mix_kernel(count, core_ref, sums_ref, grad_ref, momentum_ref, got_ref, out_ref, factor_ref):
    groups = grad_ref.shape[0]
    half = grad_ref.shape[1] // 2
    core = core_ref[0]
    total = jnp.sum(sums_ref[:, 0, :], axis=0, keepdims=True)[:, :1]
    factor = jnp.minimum(1.0, 0.5 / jnp.sqrt(total / count + 1e-06))
    factor_ref[...] = jnp.broadcast_to(factor, factor_ref.shape)
    rows = pl.ds(pl.multiple_of(core * half, half), half)
    mine = core * groups
    theirs = (1 - core) * groups

    def mix(g, m):
        clipped = g * factor
        return clipped + 0.95 * (0.95 * m + clipped)

    for i in range(groups):
        out_ref[mine + i] = mix(grad_ref[i, rows, :].astype(F32), momentum_ref[i, rows, :])
        out_ref[theirs + i] = mix(got_ref[0, i], got_ref[1, i])


def gram_kernel(x_ref, g_ref, xh, xl, th, tl):
    split_both_ways(x_ref, xh, xl, th, tl)
    for i, j in PAIRS:
        g_ref[blk(i), blk(j)] = dot3(th[blk(i), :], tl[blk(i), :], xh[:, blk(j)], xl[:, blk(j)])


def poly_kernel(xh, xl, part_ref, other_ref, out_ref, raw, yh, yl, th, tl, gh, gl, mh, ml, ph, pl_):
    split_both_ways(other_ref, yh, yl, th, tl)
    shape = (BLOCK, BLOCK)
    eye = (lax.broadcasted_iota(jnp.int32, shape, 0) == lax.broadcasted_iota(jnp.int32, shape, 1)).astype(F32)
    trace = jnp.zeros((1, 1), F32)
    for i, j in PAIRS:
        v = part_ref[blk(i), blk(j)] + dot3(th[blk(i), :], tl[blk(i), :], yh[:, blk(j)], yl[:, blk(j)])
        raw[blk(i), blk(j)] = v
        if i == j:
            trace = trace + jnp.sum(jnp.sum(v * eye, axis=0, keepdims=True), axis=1, keepdims=True)
    inverse = 1.0 / (jnp.sqrt(trace) + 1e-07)
    for i, j in PAIRS:
        v = raw[blk(i), blk(j)] * inverse * inverse
        raw[blk(i), blk(j)] = v
        put_symmetric(gh, gl, i, j, v)

    def polynomial(h, l, oh, ol):
        for i, j in PAIRS:
            v = A1 * raw[blk(i), blk(j)] + A2 * dot3(h[blk(i), :], l[blk(i), :], h[:, blk(j)], l[:, blk(j)])
            if i == j:
                v = v + A0 * eye
            put_symmetric(oh, ol, i, j, v)

    polynomial(gh, gl, mh, ml)
    for i, j in PAIRS:
        put_symmetric(ph, pl_, i, j, dot3(gh[blk(i), :], gl[blk(i), :], mh[:, blk(j)], ml[:, blk(j)]))
    rows = range(out_ref.shape[0] // BLOCK)
    for i in rows:
        for j in range(NB):
            v = dot3(xh[blk(i), :], xl[blk(i), :], mh[:, blk(j)], ml[:, blk(j)]) * inverse
            yh[blk(i), blk(j)], yl[blk(i), blk(j)] = split(v)
    for i, j in PAIRS:
        v = dot3(ph[blk(i), :], pl_[blk(i), :], mh[:, blk(j)], ml[:, blk(j)])
        raw[blk(i), blk(j)] = v
        put_symmetric(gh, gl, i, j, v)
    polynomial(gh, gl, ph, pl_)
    scale = 0.2 * math.sqrt(max(R, C))
    for i in rows:
        for j in range(NB):
            out_ref[blk(i), blk(j)] = scale * dot3(yh[blk(i), :], yl[blk(i), :], ph[:, blk(j)], pl_[:, blk(j)])


def orthogonalize(own, other):
    n = own.shape[0]
    wide, tall, square = ((n, C), (C, n), (C, C))
    part, xh, xl = pl.pallas_call(
        gram_kernel,
        out_shape=(
            jax.ShapeDtypeStruct(square, F32),
            jax.ShapeDtypeStruct(wide, BF16),
            jax.ShapeDtypeStruct(wide, BF16),
        ),
        in_specs=[VMEM],
        out_specs=(VMEM,) * 3,
        scratch_shapes=[pltpu.VMEM(tall, BF16)] * 2,
        compiler_params=params(12),
        name="gram",
    )(own)
    return pl.pallas_call(
        poly_kernel,
        out_shape=jax.ShapeDtypeStruct(wide, F32),
        in_specs=[VMEM] * 4,
        out_specs=VMEM,
        scratch_shapes=[pltpu.VMEM(square, F32)]
        + [pltpu.VMEM(wide, BF16)] * 2
        + [pltpu.VMEM(tall, BF16)] * 2
        + [pltpu.VMEM(square, BF16)] * 6,
        compiler_params=params(24),
        name="poly",
    )(xh, xl, part, other)


def body(grad, momentum):
    groups, slice_rows, columns = grad.shape
    n_rows = lax.axis_size("dp")
    devices = n_rows * lax.axis_size("expert")
    core = lax.axis_index("expert") % 2
    half = slice_rows // 2
    count = groups * slice_rows * columns * devices

    core_index = core.reshape(1)
    tile, give = pl.pallas_call(
        prepare_kernel,
        out_shape=(
            jax.ShapeDtypeStruct((devices, 1, 128), F32),
            jax.ShapeDtypeStruct((2, groups, half, columns), F32),
        ),
        in_specs=[SMEM] + [VMEM] * 2,
        out_specs=(VMEM, VMEM),
        compiler_params=params(8),
        name="prepare",
    )(core_index, grad, momentum)
    sums = lax.all_to_all(tile, ("dp", "expert"), split_axis=0, concat_axis=0, tiled=True)
    got = swap_cores(give)
    outgoing, factor = pl.pallas_call(
        lambda *refs: mix_kernel(count, *refs),
        out_shape=(
            jax.ShapeDtypeStruct((n_rows, half, columns), F32),
            jax.ShapeDtypeStruct((8, 128), F32),
        ),
        in_specs=[SMEM] + [VMEM] * 4,
        out_specs=(VMEM, VMEM),
        compiler_params=params(10),
        name="mix",
    )(core_index, sums, grad, momentum, got)

    own = lax.all_to_all(outgoing, "dp", split_axis=0, concat_axis=0, tiled=True)
    factor, grad, momentum, own = lax.optimization_barrier((factor, grad, momentum, own))
    new_momentum = pl.pallas_call(
        momentum_kernel,
        out_shape=jax.ShapeDtypeStruct(momentum.shape, F32),
        in_specs=[VMEM] * 3,
        out_specs=VMEM,
        compiler_params=params(8),
        name="momentum",
    )(factor, grad, momentum)
    own = own.reshape(n_rows * half, columns)
    finished = orthogonalize(own, swap_cores(own))

    finished, new_momentum = lax.optimization_barrier((finished, new_momentum))
    back = lax.all_to_all(
        finished.reshape(n_rows, half, columns), "dp", split_axis=0, concat_axis=0, tiled=True
    )
    theirs = lax.dynamic_slice_in_dim(back, (1 - core) * groups, groups, 0)
    got = swap_cores(theirs)
    update = place(True, core_index, back, grad.shape)
    update = place(False, core_index, got, grad.shape, (update,))
    return (new_momentum, update)


def solution(mesh):
    in_specs = (P("expert", "dp", None), P("expert", "dp", None))
    out_specs = (P("expert", "dp", None), P("expert", "dp", None))
    return jax.shard_map(body, mesh=mesh, in_specs=in_specs, out_specs=out_specs, check_vma=False)
```

time: 162 us -> 142 us (0.88)
  matrix products: 25.4 us -> 0 us
  waiting for transfers between devices: 16.7 us -> 38.9 us
  blocking collectives: 86.3 us -> 66.3 us
  Pallas kernels: 0 us -> 19.6 us
  other arithmetic: 9.61 us -> 0 us
  starting transfers between devices: 19.6 us -> 13.3 us
  between operations: 2.73 us -> 0.86 us
    dot_general x8 -> x0, matrix products: 25.4 us -> none  [the longest x6 17.6 us: mm(): jnp.dot(a, b, precision=lax.Precision.HIGH, preferred_element_type=jnp.fl...]
    all_to_all x1, waiting for transfers between devices: 12.9 us -> 37.7 us  [body(): lax.all_to_all(finished.reshape(n_rows, half, columns), 'dp', split_axis=...]
    pallas_call x0 -> x7, Pallas kernels: none -> 19.6 us  [the longest x1 14.2 us: orthogonalize(): pl.pallas_call(poly_kernel, out_shape=jax.ShapeDtypeStruct(wide, F32), in...]
    all_to_all x1, blocking collectives: 44 us -> 25.3 us  [body(): lax.all_to_all(tile, ('dp', 'expert'), split_axis=0, concat_axis=0, tiled...]
    all_to_all x1, starting transfers between devices: 15.7 us -> 4.36 us  [body(): lax.all_to_all(finished.reshape(n_rows, half, columns), 'dp', split_axis=...]
    reduce_sum x4 -> x0, other arithmetic: 5.01 us -> none  [the longest x1 2.14 us: body(): total = global_sum(jnp.sum(widened * widened))]
    ppermute x3, starting transfers between devices: 3.97 us -> 8.97 us  [swap_cores(): return lax.ppermute(x, 'expert', [(i, i ^ 1) for i in range(n)])]
    add x1 -> x0, other arithmetic: 3.15 us -> none  [body(): advance = clipped + 0.95 * new_momentum]
  transfers between devices with their start and end apart: 4 -> 4, of which waited for: 3 -> 3; matrix products, arithmetic and copies ran while one was open for 3% -> 0% of each run, Pallas kernels for 0% -> 3%
where the time goes in v1:
time: 142 us
  blocking collectives  66.3 us (47%)
  waiting for transfers between devices  38.9 us (27%)
  Pallas kernels  19.6 us (14%)
  starting transfers between devices  13.3 us (9%)
  local copies, waits for them, and re-layouts  2.59 us (2%)
    all_to_all x1, blocking collectives, body(): lax.all_to_all(outgoing, 'dp', split_axis=0, concat_axis=0, tiled=True)  41 us
    all_to_all x1, waiting for transfers between devices, body(): lax.all_to_all(finished.reshape(n_rows, half, columns), 'dp', split_axis=...  37.7 us
    all_to_all x1, blocking collectives, body(): lax.all_to_all(tile, ('dp', 'expert'), split_axis=0, concat_axis=0, tiled...  25.3 us
    pallas_call x1, Pallas kernels, orthogonalize(): pl.pallas_call(poly_kernel, out_shape=jax.ShapeDtypeStruct(wide, F32), in...  14.2 us
    ppermute x3, starting transfers between devices, swap_cores(): return lax.ppermute(x, 'expert', [(i, i ^ 1) for i in range(n)])  8.97 us
    all_to_all x1, starting transfers between devices, body(): lax.all_to_all(finished.reshape(n_rows, half, columns), 'dp', split_axis=...  4.36 us
  transfers between devices with their start and end apart: 4, of which 3 were waited for; matrix products, arithmetic and copies ran while one was open for 0% of the time, Pallas kernels for 3%

profile of v1, /device:TPU:1, one launch (start us, length us, event | category | flops | bytes accessed | tf_op | source)
XLA Modules:
  0.0 141.6 jit_solution(502085766652336684)
XLA Ops:
  0.6 0.0 copy-start
  0.6 1.4 copy-done
  2.0 0.0 copy-start.2
  2.1 1.1 copy-done.2
  3.2 0.3 prepare.1
  3.5 3.3 %collective-permute-start = (f32[2,16,16,768]{3,2,1,0:T(8,128)S(1)}, f32[2,16,16,768]{3,2,1,0:T(8,128)S(1)}, u32[]{:S(2)}, u32[]{:S(2)}) collective-permute-start(f32[2,16,16,768]{3,2,1,0:T(8,128)S(1)} %get-tuple-element.16), channel_id=1, source_target_pairs={{0,1},{1,0},{2,3},{3,2},{4,5},{5,4},{6,7},{7,6},{8,9},{9,8},{10,11... | collective-permute-start | bytes 4718600 | tf_op jit(solution)/shard_map/ppermute | solution.py:32
  6.9 25.3 %all_to_all.15.refs_1_ = f32[256,1,128]{2,1,0:T(1,128)S(1)} all-to-all(f32[256,1,128]{2,1,0:T(1,128)S(1)} %get-tuple-element.15), channel_id=1, replica_groups=mesh['dp'=32,'expert'=8] {'dp','expert'}, dimensions={0} | all-to-all | bytes 262144 | tf_op jit(solution)/shard_map/all_to_all | solution.py:227
  32.2 0.0 collective-permute-done.refs_4_
  32.2 0.0 copy-done.1
  32.2 0.0 copy-done.3
  32.2 0.5 mix.1
  32.7 41.0 %all_to_all.16 = f32[32,16,768]{2,1,0:T(8,128)S(1)} all-to-all(f32[32,16,768]{2,1,0:T(8,128)S(1)} %get-tuple-element.18), channel_id=1, replica_groups=mesh['dp'=32,'expert'=8] {'dp'}, dimensions={0} | all-to-all | bytes 3145728 | tf_op jit(solution)/shard_map/all_to_all | solution.py:241
  73.7 3.2 %collective-permute-start.1 = (f32[512,768]{1,0:T(8,128)S(1)}, f32[512,768]{1,0:T(8,128)S(1)}, u32[]{:S(2)}, u32[]{:S(2)}) collective-permute-start(f32[512,768]{1,0:T(8,128)S(1)} %bitcast.3), channel_id=1, source_target_pairs={{0,1},{1,0},{2,3},{3,2},{4,5},{5,4},{6,7},{7,6},{8,9},{9,8},{10,11... | collective-permute-start | bytes 4718600 | tf_op jit(solution)/shard_map/ppermute | solution.py:32
  76.9 1.5 %gram.1 = (f32[768,768]{1,0:T(8,128)S(1)}, bf16[512,768]{1,0:T(8,128)(2,1)S(1)}, bf16[512,768]{1,0:T(8,128)(2,1)S(1)}) custom-call(f32[512,768]{1,0:T(8,128)S(1)} %bitcast.4), custom_call_target="tpu_custom_call" | custom-call | tf_op jit(solution)/shard_map/gram/pallas_call | solution.py:180
  78.4 1.4 momentum.1
  79.8 0.2 collective-permute-done.1.other_ref
  79.9 14.2 %poly.1 = f32[512,768]{1,0:T(8,128)} custom-call(bf16[512,768]{1,0:T(8,128)(2,1)S(1)} %get-tuple-element.20.xh, bf16[512,768]{1,0:T(8,128)(2,1)S(1)} %get-tuple-element.21.xl, f32[768,768]{1,0:T(8,128)S(1)} %get-tuple-element.22.part_ref, f32[512,768]{1,0:T(8,128)S(1)} %collective-permute-done.1.other_ref), custom_call_target="tpu_custom_call" | custom-call | tf_op jit(solution)/shard_map/poly/pallas_call | solution.py:193
  94.1 4.4 %all-to-all-start.2 = ((f32[32,16,768]{2,1,0:T(8,128)}), f32[32,16,768]{2,1,0:T(8,128)S(1)}, u32[]{:S(2)}, u32[]{:S(2)}) async-start(f32[32,16,768]{2,1,0:T(8,128)} %bitcast.2), calls=%async_computation.2 | async-start | bytes 3145728 | tf_op jit(solution)/shard_map/all_to_all | solution.py:255
  98.5 37.7 %all-to-all-done.2.refs_1_ = f32[32,16,768]{2,1,0:T(8,128)S(1)} async-done(((f32[32,16,768]{2,1,0:T(8,128)}), f32[32,16,768]{2,1,0:T(8,128)S(1)}, u32[]{:S(2)}, u32[]{:S(2)}) %all-to-all-start.2) | async-done | bytes 1572896 | tf_op jit(solution)/shard_map/all_to_all | solution.py:255
  136.2 0.1 constant_dynamic-slice_fusion
  136.3 2.4 %collective-permute-start.2 = (f32[16,16,768]{2,1,0:T(8,128)S(1)}, f32[16,16,768]{2,1,0:T(8,128)S(1)}, u32[]{:S(2)}, u32[]{:S(2)}) collective-permute-start(f32[16,16,768]{2,1,0:T(8,128)S(1)} %constant_dynamic-slice_fusion), channel_id=1, source_target_pairs={{0,1},{1,0},{2,3},{3,2},{4,5},{5,4},{6,7},{7,6},{8,9},{9,8},{10,11... | collective-permute-start | bytes 2359304 | tf_op jit(solution)/shard_map/ppermute | solution.py:32
  138.7 0.9 place.2.refs_2_
  139.6 1.0 collective-permute-done.2.refs_1_
  140.6 0.9 place.3
  (2 shorter events, 0.0 us)
Async XLA Ops:
  0.6 1.4 copy-start
  2.0 1.1 copy-start.2
  3.2 29.0 %copy-start.1 = (f32[16,32,768]{2,1,0:T(8,128)S(1)}, f32[16,32,768]{2,1,0:T(8,128)}, u32[]{:S(2)}) copy-start(f32[16,32,768]{2,1,0:T(8,128)} %momentum_ref.2) | copy-start | bytes 4718596
  3.2 29.0 %copy-start.3 = (bf16[16,32,768]{2,1,0:T(8,128)(2,1)S(1)}, bf16[16,32,768]{2,1,0:T(8,128)(2,1)}, u32[]{:S(2)}) copy-start(bf16[16,32,768]{2,1,0:T(8,128)(2,1)} %grad_ref.2) | copy-start | bytes 2359300
  3.5 28.7 %collective-permute-start = (f32[2,16,16,768]{3,2,1,0:T(8,128)S(1)}, f32[2,16,16,768]{3,2,1,0:T(8,128)S(1)}, u32[]{:S(2)}, u32[]{:S(2)}) collective-permute-start(f32[2,16,16,768]{3,2,1,0:T(8,128)S(1)} %get-tuple-element.16), channel_id=1, source_target_pairs={{0,1},{1,0},{2,3},{3,2},{4,5},{5,4},{6,7},{7,6},{8,9},{9,8},{10,11... | collective-permute-start | bytes 4718600 | tf_op jit(solution)/shard_map/ppermute | solution.py:32
  73.7 6.3 %collective-permute-start.1 = (f32[512,768]{1,0:T(8,128)S(1)}, f32[512,768]{1,0:T(8,128)S(1)}, u32[]{:S(2)}, u32[]{:S(2)}) collective-permute-start(f32[512,768]{1,0:T(8,128)S(1)} %bitcast.3), channel_id=1, source_target_pairs={{0,1},{1,0},{2,3},{3,2},{4,5},{5,4},{6,7},{7,6},{8,9},{9,8},{10,11... | collective-permute-start | bytes 4718600 | tf_op jit(solution)/shard_map/ppermute | solution.py:32
  94.1 42.1 %all-to-all-start.2 = ((f32[32,16,768]{2,1,0:T(8,128)}), f32[32,16,768]{2,1,0:T(8,128)S(1)}, u32[]{:S(2)}, u32[]{:S(2)}) async-start(f32[32,16,768]{2,1,0:T(8,128)} %bitcast.2), calls=%async_computation.2 | async-start | bytes 3145728 | tf_op jit(solution)/shard_map/all_to_all | solution.py:255
  136.3 4.3 %collective-permute-start.2 = (f32[16,16,768]{2,1,0:T(8,128)S(1)}, f32[16,16,768]{2,1,0:T(8,128)S(1)}, u32[]{:S(2)}, u32[]{:S(2)}) collective-permute-start(f32[16,16,768]{2,1,0:T(8,128)S(1)} %constant_dynamic-slice_fusion), channel_id=1, source_target_pairs={{0,1},{1,0},{2,3},{3,2},{4,5},{5,4},{6,7},{7,6},{8,9},{9,8},{10,11... | collective-permute-start | bytes 2359304 | tf_op jit(solution)/shard_map/ppermute | solution.py:32

commit v2 on v1

--- a/solution.py
+++ b/solution.py
@@ -21,6 +21,7 @@
 VMEM = pl.BlockSpec(memory_space=pltpu.VMEM)
 SMEM = pl.BlockSpec(memory_space=pltpu.SMEM)
 HBM = pl.BlockSpec(memory_space=pl.ANY)
+PINNED = pl.BlockSpec(memory_space=pltpu.HBM)
 
 
 def params(mib):
@@ -47,6 +48,13 @@
 
 def blk(i):
     return pl.ds(i * BLOCK, BLOCK)
+
+
+def square(rh, rl, ch, cl, i, j):
+    if i != j:
+        return dot3(rh[blk(i), :], rl[blk(i), :], ch[:, blk(j)], cl[:, blk(j)])
+    cross = dot(rh[blk(i), :], cl[:, blk(j)])
+    return dot(rh[blk(i), :], ch[:, blk(j)]) + (cross + cross.T)
 
 
 def put_symmetric(h, l, i, j, v):
@@ -62,23 +70,44 @@
         th[blk(j), :], tl[blk(j), :] = split(v.T)
 
 
-def prepare_kernel(core_ref, grad_ref, momentum_ref, sum_ref, give_ref):
-    half = grad_ref.shape[1] // 2
-    rows = pl.ds(pl.multiple_of((1 - core_ref[0]) * half, half), half)
-    total = jnp.zeros(grad_ref.shape[1:], F32)
-    for i in range(grad_ref.shape[0]):
-        v = grad_ref[i].astype(F32)
-        total = total + v * v
-        give_ref[0, i] = grad_ref[i, rows, :].astype(F32)
-        give_ref[1, i] = momentum_ref[i, rows, :]
+def halves(core_ref, slice_rows):
+    half = slice_rows // 2
+    core = core_ref[0]
+    return (
+        pl.ds(pl.multiple_of(core * half, half), half),
+        pl.ds(pl.multiple_of((1 - core) * half, half), half),
+    )
+
+
+def prepare_kernel(core_ref, grad_ref, momentum_ref, sum_ref, keep_ref, give_ref, wide, sems):
+    keep, give = halves(core_ref, grad_ref.shape[1])
+    copies = [
+        pltpu.make_async_copy(grad_ref, wide, sems.at[0]),
+        pltpu.make_async_copy(momentum_ref.at[:, give, :], give_ref.at[1], sems.at[1]),
+        pltpu.make_async_copy(momentum_ref.at[:, keep, :], keep_ref.at[1], sems.at[2]),
+    ]
+    for copy in copies:
+        copy.start()
+    copies[0].wait()
+    total = jnp.zeros(give_ref.shape[2:], F32)
+    for i in range(wide.shape[0]):
+        kept = wide[i, keep, :].astype(F32)
+        given = wide[i, give, :].astype(F32)
+        total = total + kept * kept + given * given
+        keep_ref[0, i] = kept
+        give_ref[0, i] = given
     total = jnp.sum(jnp.sum(total, axis=0, keepdims=True), axis=1, keepdims=True)
     sum_ref[...] = jnp.broadcast_to(total[None], sum_ref.shape)
-
-
-def momentum_kernel(factor_ref, grad_ref, momentum_ref, out_ref):
+    for copy in copies[1:]:
+        copy.wait()
+
+
+def momentum_kernel(core_ref, factor_ref, keep_ref, give_ref, out_ref):
     factor = factor_ref[:1, :1]
-    for i in range(grad_ref.shape[0]):
-        out_ref[i] = 0.95 * momentum_ref[i] + grad_ref[i].astype(F32) * factor
+    keep, give = halves(core_ref, out_ref.shape[1])
+    for i in range(out_ref.shape[0]):
+        out_ref[i, keep, :] = 0.95 * keep_ref[1, i] + keep_ref[0, i] * factor
+        out_ref[i, give, :] = 0.95 * give_ref[1, i] + give_ref[0, i] * factor
 
 
 def place_kernel(of_core, core_ref, values_ref, *refs):
@@ -106,39 +135,36 @@
     )(core, values, *before)
 
 
-def mix_kernel(count, core_ref, sums_ref, grad_ref, momentum_ref, got_ref, out_ref, factor_ref):
-    groups = grad_ref.shape[0]
-    half = grad_ref.shape[1] // 2
-    core = core_ref[0]
+def mix_kernel(count, core_ref, sums_ref, keep_ref, got_ref, out_ref, factor_ref):
+    groups = keep_ref.shape[1]
     total = jnp.sum(sums_ref[:, 0, :], axis=0, keepdims=True)[:, :1]
     factor = jnp.minimum(1.0, 0.5 / jnp.sqrt(total / count + 1e-06))
     factor_ref[...] = jnp.broadcast_to(factor, factor_ref.shape)
-    rows = pl.ds(pl.multiple_of(core * half, half), half)
-    mine = core * groups
-    theirs = (1 - core) * groups
+    mine = core_ref[0] * groups
+    theirs = (1 - core_ref[0]) * groups
 
     def mix(g, m):
         clipped = g * factor
         return clipped + 0.95 * (0.95 * m + clipped)
 
     for i in range(groups):
-        out_ref[mine + i] = mix(grad_ref[i, rows, :].astype(F32), momentum_ref[i, rows, :])
+        out_ref[mine + i] = mix(keep_ref[0, i], keep_ref[1, i])
         out_ref[theirs + i] = mix(got_ref[0, i], got_ref[1, i])
 
 
 def gram_kernel(x_ref, g_ref, xh, xl, th, tl):
     split_both_ways(x_ref, xh, xl, th, tl)
     for i, j in PAIRS:
-        g_ref[blk(i), blk(j)] = dot3(th[blk(i), :], tl[blk(i), :], xh[:, blk(j)], xl[:, blk(j)])
-
-
-def poly_kernel(xh, xl, part_ref, other_ref, out_ref, raw, yh, yl, th, tl, gh, gl, mh, ml, ph, pl_):
+        g_ref[blk(i), blk(j)] = square(th, tl, xh, xl, i, j)
+
+
+def poly_kernel(xh, xl, part_ref, other_ref, out_ref, raw, yh, yl, th, tl, gh, gl, mh, ml, nh, nl):
     split_both_ways(other_ref, yh, yl, th, tl)
     shape = (BLOCK, BLOCK)
     eye = (lax.broadcasted_iota(jnp.int32, shape, 0) == lax.broadcasted_iota(jnp.int32, shape, 1)).astype(F32)
     trace = jnp.zeros((1, 1), F32)
     for i, j in PAIRS:
-        v = part_ref[blk(i), blk(j)] + dot3(th[blk(i), :], tl[blk(i), :], yh[:, blk(j)], yl[:, blk(j)])
+        v = part_ref[blk(i), blk(j)] + square(th, tl, yh, yl, i, j)
         raw[blk(i), blk(j)] = v
         if i == j:
             trace = trace + jnp.sum(jnp.sum(v * eye, axis=0, keepdims=True), axis=1, keepdims=True)
@@ -150,28 +176,28 @@
 
     def polynomial(h, l, oh, ol):
         for i, j in PAIRS:
-            v = A1 * raw[blk(i), blk(j)] + A2 * dot3(h[blk(i), :], l[blk(i), :], h[:, blk(j)], l[:, blk(j)])
+            v = A1 * raw[blk(i), blk(j)] + A2 * square(h, l, h, l, i, j)
             if i == j:
                 v = v + A0 * eye
             put_symmetric(oh, ol, i, j, v)
 
     polynomial(gh, gl, mh, ml)
     for i, j in PAIRS:
-        put_symmetric(ph, pl_, i, j, dot3(gh[blk(i), :], gl[blk(i), :], mh[:, blk(j)], ml[:, blk(j)]))
+        put_symmetric(nh, nl, i, j, square(mh, ml, mh, ml, i, j))
     rows = range(out_ref.shape[0] // BLOCK)
     for i in rows:
         for j in range(NB):
             v = dot3(xh[blk(i), :], xl[blk(i), :], mh[:, blk(j)], ml[:, blk(j)]) * inverse
             yh[blk(i), blk(j)], yl[blk(i), blk(j)] = split(v)
     for i, j in PAIRS:
-        v = dot3(ph[blk(i), :], pl_[blk(i), :], mh[:, blk(j)], ml[:, blk(j)])
+        v = dot3(gh[blk(i), :], gl[blk(i), :], nh[:, blk(j)], nl[:, blk(j)])
         raw[blk(i), blk(j)] = v
-        put_symmetric(gh, gl, i, j, v)
-    polynomial(gh, gl, ph, pl_)
+        put_symmetric(mh, ml, i, j, v)
+    polynomial(mh, ml, nh, nl)
     scale = 0.2 * math.sqrt(max(R, C))
     for i in rows:
         for j in range(NB):
-            out_ref[blk(i), blk(j)] = scale * dot3(yh[blk(i), :], yl[blk(i), :], ph[:, blk(j)], pl_[:, blk(j)])
+            out_ref[blk(i), blk(j)] = scale * dot3(yh[blk(i), :], yl[blk(i), :], nh[:, blk(j)], nl[:, blk(j)])
 
 
 def orthogonalize(own, other):
@@ -213,17 +239,20 @@
     count = groups * slice_rows * columns * devices
 
     core_index = core.reshape(1)
-    tile, give = pl.pallas_call(
+    pair = jax.ShapeDtypeStruct((2, groups, half, columns), F32)
+    tile, keep, give = pl.pallas_call(
         prepare_kernel,
-        out_shape=(
-            jax.ShapeDtypeStruct((devices, 1, 128), F32),
-            jax.ShapeDtypeStruct((2, groups, half, columns), F32),
-        ),
-        in_specs=[SMEM] + [VMEM] * 2,
-        out_specs=(VMEM, VMEM),
+        out_shape=(jax.ShapeDtypeStruct((devices, 1, 128), F32), pair, pair),
+        in_specs=[SMEM] + [PINNED] * 2,
+        out_specs=(VMEM,) * 3,
+        scratch_shapes=[pltpu.VMEM(grad.shape, grad.dtype), pltpu.SemaphoreType.DMA((3,))],
         compiler_params=params(8),
         name="prepare",
-    )(core_index, grad, momentum)
+    )(
+        core_index,
+        pltpu.with_memory_space_constraint(grad, pltpu.HBM),
+        pltpu.with_memory_space_constraint(momentum, pltpu.HBM),
+    )
     sums = lax.all_to_all(tile, ("dp", "expert"), split_axis=0, concat_axis=0, tiled=True)
     got = swap_cores(give)
     outgoing, factor = pl.pallas_call(
@@ -232,22 +261,22 @@
             jax.ShapeDtypeStruct((n_rows, half, columns), F32),
             jax.ShapeDtypeStruct((8, 128), F32),
         ),
-        in_specs=[SMEM] + [VMEM] * 4,
+        in_specs=[SMEM] + [VMEM] * 3,
         out_specs=(VMEM, VMEM),
         compiler_params=params(10),
         name="mix",
-    )(core_index, sums, grad, momentum, got)
+    )(core_index, sums, keep, got)
 
     own = lax.all_to_all(outgoing, "dp", split_axis=0, concat_axis=0, tiled=True)
-    factor, grad, momentum, own = lax.optimization_barrier((factor, grad, momentum, own))
+    factor, keep, give, own = lax.optimization_barrier((factor, keep, give, own))
     new_momentum = pl.pallas_call(
         momentum_kernel,
         out_shape=jax.ShapeDtypeStruct(momentum.shape, F32),
-        in_specs=[VMEM] * 3,
+        in_specs=[SMEM] + [VMEM] * 3,
         out_specs=VMEM,
         compiler_params=params(8),
         name="momentum",
-    )(factor, grad, momentum)
+    )(core_index, factor, keep, give)
     own = own.reshape(n_rows * half, columns)
     finished = orthogonalize(own, swap_cores(own))
 

time: 142 us -> 140 us (0.986)
  local copies, waits for them, and re-layouts: 2.59 us -> 0.05 us
    unnamed x8 -> x0, local copies, waits for them, and re-layouts: 2.54 us -> none
where the time goes in v2:
time: 140 us; the launch traced here: 139 us
  blocking collectives  66.3 us (47%)
  waiting for transfers between devices  39.1 us (28%)
  Pallas kernels  19.7 us (14%)
  starting transfers between devices  13.3 us (10%)
    all_to_all x1, blocking collectives, body(): lax.all_to_all(outgoing, 'dp', split_axis=0, concat_axis=0, tiled=True)  41 us
    all_to_all x1, waiting for transfers between devices, body(): lax.all_to_all(finished.reshape(n_rows, half, columns), 'dp', split_axis=...  37.7 us
    all_to_all x1, blocking collectives, body(): lax.all_to_all(tile, ('dp', 'expert'), split_axis=0, concat_axis=0, tiled...  25.3 us
    pallas_call x1, Pallas kernels, orthogonalize(): pl.pallas_call(poly_kernel, out_shape=jax.ShapeDtypeStruct(wide, F32), in...  13.1 us
    ppermute x3, starting transfers between devices, swap_cores(): return lax.ppermute(x, 'expert', [(i, i ^ 1) for i in range(n)])  8.98 us
    all_to_all x1, starting transfers between devices, body(): lax.all_to_all(finished.reshape(n_rows, half, columns), 'dp', split_axis=...  4.35 us
  transfers between devices with their start and end apart: 4, of which 3 were waited for; matrix products, arithmetic and copies ran while one was open for 0% of the time, Pallas kernels for 3%

profile of v2, /device:TPU:1, one launch (start us, length us, event | category | flops | bytes accessed | tf_op | source)
XLA Modules:
  0.0 139.3 jit_solution(6338868088506982035)
XLA Ops:
  0.6 1.6 %prepare.1 = (f32[256,1,128]{2,1,0:T(1,128)S(1)}, f32[2,16,16,768]{3,2,1,0:T(8,128)S(1)}, f32[2,16,16,768]{3,2,1,0:T(8,128)S(1)}) custom-call(s32[1]{0:T(128)} %bitcast.core_ref.refs_0_, bf16[16,32,768]{2,1,0:T(8,128)(2,1)} %grad_ref.1, f32[16,32,768]{2,1,0:T(8,128)} %momentum_ref.1), custom_call_target="tpu_custom_call" | custom-call | tf_op jit(solution)/shard_map/prepare/pallas_call | solution.py:243
  2.3 3.3 %collective-permute-start = (f32[2,16,16,768]{3,2,1,0:T(8,128)S(1)}, f32[2,16,16,768]{3,2,1,0:T(8,128)S(1)}, u32[]{:S(2)}, u32[]{:S(2)}) collective-permute-start(f32[2,16,16,768]{3,2,1,0:T(8,128)S(1)} %get-tuple-element.27.give_ref), channel_id=1, source_target_pairs={{0,1},{1,0},{2,3},{3,2},{4,5},{5,4},{6,7},{7,6},{8,9},{9,8},{10,11... | collective-permute-start | bytes 4718600 | tf_op jit(solution)/shard_map/ppermute | solution.py:33
  5.6 25.3 %all_to_all.15.refs_1_ = f32[256,1,128]{2,1,0:T(1,128)S(1)} all-to-all(f32[256,1,128]{2,1,0:T(1,128)S(1)} %get-tuple-element.16), channel_id=1, replica_groups=mesh['dp'=32,'expert'=8] {'dp','expert'}, dimensions={0} | all-to-all | bytes 262144 | tf_op jit(solution)/shard_map/all_to_all | solution.py:256
  30.9 0.0 collective-permute-done.refs_3_
  30.9 0.5 mix.1
  31.4 41.0 %all_to_all.16 = f32[32,16,768]{2,1,0:T(8,128)S(1)} all-to-all(f32[32,16,768]{2,1,0:T(8,128)S(1)} %get-tuple-element.20), channel_id=1, replica_groups=mesh['dp'=32,'expert'=8] {'dp'}, dimensions={0} | all-to-all | bytes 3145728 | tf_op jit(solution)/shard_map/all_to_all | solution.py:270
  72.4 3.3 %collective-permute-start.1 = (f32[512,768]{1,0:T(8,128)S(1)}, f32[512,768]{1,0:T(8,128)S(1)}, u32[]{:S(2)}, u32[]{:S(2)}) collective-permute-start(f32[512,768]{1,0:T(8,128)S(1)} %bitcast.3), channel_id=1, source_target_pairs={{0,1},{1,0},{2,3},{3,2},{4,5},{5,4},{6,7},{7,6},{8,9},{9,8},{10,11... | collective-permute-start | bytes 4718600 | tf_op jit(solution)/shard_map/ppermute | solution.py:33
  75.6 1.3 gram.1
  76.9 1.4 momentum.1
  78.3 0.4 collective-permute-done.1.other_ref
  78.7 13.1 %poly.1 = f32[512,768]{1,0:T(8,128)} custom-call(bf16[512,768]{1,0:T(8,128)(2,1)S(1)} %get-tuple-element.22.xh, bf16[512,768]{1,0:T(8,128)(2,1)S(1)} %get-tuple-element.23.xl, f32[768,768]{1,0:T(8,128)S(1)} %get-tuple-element.24.part_ref, f32[512,768]{1,0:T(8,128)S(1)} %collective-permute-done.1.other_ref), custom_call_target="tpu_custom_call" | custom-call | tf_op jit(solution)/shard_map/poly/pallas_call | solution.py:219
  91.8 4.4 %all-to-all-start.2 = ((f32[32,16,768]{2,1,0:T(8,128)}), f32[32,16,768]{2,1,0:T(8,128)S(1)}, u32[]{:S(2)}, u32[]{:S(2)}) async-start(f32[32,16,768]{2,1,0:T(8,128)} %bitcast.2), calls=%async_computation.2 | async-start | bytes 3145728 | tf_op jit(solution)/shard_map/all_to_all | solution.py:284
  96.2 37.7 %all-to-all-done.2.refs_1_ = f32[32,16,768]{2,1,0:T(8,128)S(1)} async-done(((f32[32,16,768]{2,1,0:T(8,128)}), f32[32,16,768]{2,1,0:T(8,128)S(1)}, u32[]{:S(2)}, u32[]{:S(2)}) %all-to-all-start.2) | async-done | bytes 1572896 | tf_op jit(solution)/shard_map/all_to_all | solution.py:284
  133.9 0.1 constant_dynamic-slice_fusion
  134.0 2.4 %collective-permute-start.2 = (f32[16,16,768]{2,1,0:T(8,128)S(1)}, f32[16,16,768]{2,1,0:T(8,128)S(1)}, u32[]{:S(2)}, u32[]{:S(2)}) collective-permute-start(f32[16,16,768]{2,1,0:T(8,128)S(1)} %constant_dynamic-slice_fusion), channel_id=1, source_target_pairs={{0,1},{1,0},{2,3},{3,2},{4,5},{5,4},{6,7},{7,6},{8,9},{9,8},{10,11... | collective-permute-start | bytes 2359304 | tf_op jit(solution)/shard_map/ppermute | solution.py:33
  136.4 0.9 place.2.refs_2_
  137.3 1.0 collective-permute-done.2.refs_1_
  138.3 0.9 place.3
Async XLA Ops:
  2.3 28.7 %collective-permute-start = (f32[2,16,16,768]{3,2,1,0:T(8,128)S(1)}, f32[2,16,16,768]{3,2,1,0:T(8,128)S(1)}, u32[]{:S(2)}, u32[]{:S(2)}) collective-permute-start(f32[2,16,16,768]{3,2,1,0:T(8,128)S(1)} %get-tuple-element.27.give_ref), channel_id=1, source_target_pairs={{0,1},{1,0},{2,3},{3,2},{4,5},{5,4},{6,7},{7,6},{8,9},{9,8},{10,11... | collective-permute-start | bytes 4718600 | tf_op jit(solution)/shard_map/ppermute | solution.py:33
  72.4 6.3 %collective-permute-start.1 = (f32[512,768]{1,0:T(8,128)S(1)}, f32[512,768]{1,0:T(8,128)S(1)}, u32[]{:S(2)}, u32[]{:S(2)}) collective-permute-start(f32[512,768]{1,0:T(8,128)S(1)} %bitcast.3), channel_id=1, source_target_pairs={{0,1},{1,0},{2,3},{3,2},{4,5},{5,4},{6,7},{7,6},{8,9},{9,8},{10,11... | collective-permute-start | bytes 4718600 | tf_op jit(solution)/shard_map/ppermute | solution.py:33
  91.8 42.1 %all-to-all-start.2 = ((f32[32,16,768]{2,1,0:T(8,128)}), f32[32,16,768]{2,1,0:T(8,128)S(1)}, u32[]{:S(2)}, u32[]{:S(2)}) async-start(f32[32,16,768]{2,1,0:T(8,128)} %bitcast.2), calls=%async_computation.2 | async-start | bytes 3145728 | tf_op jit(solution)/shard_map/all_to_all | solution.py:284
  134.0 4.3 %collective-permute-start.2 = (f32[16,16,768]{2,1,0:T(8,128)S(1)}, f32[16,16,768]{2,1,0:T(8,128)S(1)}, u32[]{:S(2)}, u32[]{:S(2)}) collective-permute-start(f32[16,16,768]{2,1,0:T(8,128)S(1)} %constant_dynamic-slice_fusion), channel_id=1, source_target_pairs={{0,1},{1,0},{2,3},{3,2},{4,5},{5,4},{6,7},{7,6},{8,9},{9,8},{10,11... | collective-permute-start | bytes 2359304 | tf_op jit(solution)/shard_map/ppermute | solution.py:33

commit v3 on v2

--- a/solution.py
+++ b/solution.py
@@ -102,37 +102,58 @@
         copy.wait()
 
 
-def momentum_kernel(core_ref, factor_ref, keep_ref, give_ref, out_ref):
+def momentum_kernel(factor_ref, grad_ref, momentum_ref, out_ref, wide, held, sems):
+    copies = [
+        pltpu.make_async_copy(grad_ref, wide, sems.at[0]),
+        pltpu.make_async_copy(momentum_ref, held, sems.at[1]),
+    ]
+    for copy in copies:
+        copy.start()
+    for copy in copies:
+        copy.wait()
     factor = factor_ref[:1, :1]
-    keep, give = halves(core_ref, out_ref.shape[1])
     for i in range(out_ref.shape[0]):
-        out_ref[i, keep, :] = 0.95 * keep_ref[1, i] + keep_ref[0, i] * factor
-        out_ref[i, give, :] = 0.95 * give_ref[1, i] + give_ref[0, i] * factor
-
-
-def place_kernel(of_core, core_ref, values_ref, *refs):
-    out_ref, sem = refs[-2:]
-    groups, slice_rows, _ = out_ref.shape
-    half = slice_rows // 2
-    core = core_ref[0] if of_core else 1 - core_ref[0]
-    source = values_ref.at[pl.ds(core * groups, groups)] if of_core else values_ref
-    rows = pl.ds(pl.multiple_of(core * half, half), half)
-    copy = pltpu.make_async_copy(source, out_ref.at[:, rows, :], sem)
+        out_ref[i] = 0.95 * held[i] + wide[i].astype(F32) * factor
+
+
+def copy_and_wait(source, target, sem):
+    copy = pltpu.make_async_copy(source, target, sem)
     copy.start()
     copy.wait()
 
 
-def place(of_core, core, values, shape, before=()):
+def place_own(core, values, shape):
+    def kernel(core_ref, values_ref, out_ref, sem):
+        keep, _ = halves(core_ref, shape[1])
+        mine = pl.ds(core_ref[0] * shape[0], shape[0])
+        copy_and_wait(values_ref.at[mine], out_ref.at[:, keep, :], sem)
+
     return pl.pallas_call(
-        lambda *refs: place_kernel(of_core, *refs),
+        kernel,
         out_shape=jax.ShapeDtypeStruct(shape, F32),
-        in_specs=[SMEM, HBM] + [HBM] * len(before),
+        in_specs=[SMEM, HBM],
         out_specs=HBM,
         scratch_shapes=[pltpu.SemaphoreType.DMA],
-        input_output_aliases={2: 0} if before else {},
         compiler_params=params(1),
-        name="place",
-    )(core, values, *before)
+        name="place_own",
+    )(core, values)
+
+
+def place_got(core, values, before):
+    def kernel(core_ref, values_ref, before_ref, out_ref, sem):
+        _, give = halves(core_ref, before.shape[1])
+        copy_and_wait(values_ref, out_ref.at[:, give, :], sem)
+
+    return pl.pallas_call(
+        kernel,
+        out_shape=jax.ShapeDtypeStruct(before.shape, F32),
+        in_specs=[SMEM, HBM, HBM],
+        out_specs=HBM,
+        scratch_shapes=[pltpu.SemaphoreType.DMA],
+        input_output_aliases={2: 0},
+        compiler_params=params(1),
+        name="place_got",
+    )(core, values, before)
 
 
 def mix_kernel(count, core_ref, sums_ref, keep_ref, got_ref, out_ref, factor_ref):
@@ -158,30 +179,36 @@
         g_ref[blk(i), blk(j)] = square(th, tl, xh, xl, i, j)
 
 
+def more_gram_kernel(x_ref, before_ref, g_ref, xh, xl, th, tl):
+    split_both_ways(x_ref, xh, xl, th, tl)
+    for i, j in PAIRS:
+        g_ref[blk(i), blk(j)] = before_ref[blk(i), blk(j)] + square(th, tl, xh, xl, i, j)
+
+
 def poly_kernel(xh, xl, part_ref, other_ref, out_ref, raw, yh, yl, th, tl, gh, gl, mh, ml, nh, nl):
-    split_both_ways(other_ref, yh, yl, th, tl)
+    some = pl.ds(0, other_ref.shape[0])
+    oh, ol = yh.at[some], yl.at[some]
+    split_both_ways(other_ref, oh, ol, th, tl)
     shape = (BLOCK, BLOCK)
     eye = (lax.broadcasted_iota(jnp.int32, shape, 0) == lax.broadcasted_iota(jnp.int32, shape, 1)).astype(F32)
     trace = jnp.zeros((1, 1), F32)
     for i, j in PAIRS:
-        v = part_ref[blk(i), blk(j)] + square(th, tl, yh, yl, i, j)
+        v = part_ref[blk(i), blk(j)] + square(th, tl, oh, ol, i, j)
         raw[blk(i), blk(j)] = v
+        put_symmetric(gh, gl, i, j, v)
         if i == j:
             trace = trace + jnp.sum(jnp.sum(v * eye, axis=0, keepdims=True), axis=1, keepdims=True)
     inverse = 1.0 / (jnp.sqrt(trace) + 1e-07)
-    for i, j in PAIRS:
-        v = raw[blk(i), blk(j)] * inverse * inverse
-        raw[blk(i), blk(j)] = v
-        put_symmetric(gh, gl, i, j, v)
-
-    def polynomial(h, l, oh, ol):
+    inverse2 = inverse * inverse
+
+    def polynomial(h, l, ph, pl_, linear, quadratic):
         for i, j in PAIRS:
-            v = A1 * raw[blk(i), blk(j)] + A2 * square(h, l, h, l, i, j)
+            v = linear * raw[blk(i), blk(j)] + quadratic * square(h, l, h, l, i, j)
             if i == j:
                 v = v + A0 * eye
-            put_symmetric(oh, ol, i, j, v)
-
-    polynomial(gh, gl, mh, ml)
+            put_symmetric(ph, pl_, i, j, v)
+
+    polynomial(gh, gl, mh, ml, A1 * inverse2, A2 * inverse2 * inverse2)
     for i, j in PAIRS:
         put_symmetric(nh, nl, i, j, square(mh, ml, mh, ml, i, j))
     rows = range(out_ref.shape[0] // BLOCK)
@@ -190,44 +217,55 @@
             v = dot3(xh[blk(i), :], xl[blk(i), :], mh[:, blk(j)], ml[:, blk(j)]) * inverse
             yh[blk(i), blk(j)], yl[blk(i), blk(j)] = split(v)
     for i, j in PAIRS:
-        v = dot3(gh[blk(i), :], gl[blk(i), :], nh[:, blk(j)], nl[:, blk(j)])
+        v = inverse2 * dot3(gh[blk(i), :], gl[blk(i), :], nh[:, blk(j)], nl[:, blk(j)])
         raw[blk(i), blk(j)] = v
         put_symmetric(mh, ml, i, j, v)
-    polynomial(mh, ml, nh, nl)
+    polynomial(mh, ml, nh, nl, A1, A2)
     scale = 0.2 * math.sqrt(max(R, C))
     for i in rows:
         for j in range(NB):
             out_ref[blk(i), blk(j)] = scale * dot3(yh[blk(i), :], yl[blk(i), :], nh[:, blk(j)], nl[:, blk(j)])
 
 
-def orthogonalize(own, other):
+def orthogonalize(own):
     n = own.shape[0]
-    wide, tall, square = ((n, C), (C, n), (C, C))
+    first, last = swap_cores(own[: n // 2]), swap_cores(own[n // 2 :])
+    wide, square_ = ((n, C), (C, C))
     part, xh, xl = pl.pallas_call(
         gram_kernel,
         out_shape=(
-            jax.ShapeDtypeStruct(square, F32),
+            jax.ShapeDtypeStruct(square_, F32),
             jax.ShapeDtypeStruct(wide, BF16),
             jax.ShapeDtypeStruct(wide, BF16),
         ),
         in_specs=[VMEM],
         out_specs=(VMEM,) * 3,
-        scratch_shapes=[pltpu.VMEM(tall, BF16)] * 2,
+        scratch_shapes=[pltpu.VMEM((C, n), BF16)] * 2,
         compiler_params=params(12),
         name="gram",
     )(own)
+    split_scratch = [pltpu.VMEM((n // 2, C), BF16)] * 2 + [pltpu.VMEM((C, n // 2), BF16)] * 2
+    part = pl.pallas_call(
+        more_gram_kernel,
+        out_shape=jax.ShapeDtypeStruct(square_, F32),
+        in_specs=[VMEM] * 2,
+        out_specs=VMEM,
+        scratch_shapes=split_scratch,
+        compiler_params=params(12),
+        name="more_gram",
+    )(first, part)
     return pl.pallas_call(
         poly_kernel,
         out_shape=jax.ShapeDtypeStruct(wide, F32),
         in_specs=[VMEM] * 4,
         out_specs=VMEM,
-        scratch_shapes=[pltpu.VMEM(square, F32)]
+        scratch_shapes=[pltpu.VMEM(square_, F32)]
         + [pltpu.VMEM(wide, BF16)] * 2
-        + [pltpu.VMEM(tall, BF16)] * 2
-        + [pltpu.VMEM(square, BF16)] * 6,
+        + split_scratch[2:]
+        + [pltpu.VMEM(square_, BF16)] * 6,
         compiler_params=params(24),
         name="poly",
-    )(xh, xl, part, other)
+    )(xh, xl, part, last)
 
 
 def body(grad, momentum):
@@ -239,6 +277,7 @@
     count = groups * slice_rows * columns * devices
 
     core_index = core.reshape(1)
+    inputs = [pltpu.with_memory_space_constraint(x, pltpu.HBM) for x in (grad, momentum)]
     pair = jax.ShapeDtypeStruct((2, groups, half, columns), F32)
     tile, keep, give = pl.pallas_call(
         prepare_kernel,
@@ -248,11 +287,7 @@
         scratch_shapes=[pltpu.VMEM(grad.shape, grad.dtype), pltpu.SemaphoreType.DMA((3,))],
         compiler_params=params(8),
         name="prepare",
-    )(
-        core_index,
-        pltpu.with_memory_space_constraint(grad, pltpu.HBM),
-        pltpu.with_memory_space_constraint(momentum, pltpu.HBM),
-    )
+    )(core_index, *inputs)
     sums = lax.all_to_all(tile, ("dp", "expert"), split_axis=0, concat_axis=0, tiled=True)
     got = swap_cores(give)
     outgoing, factor = pl.pallas_call(
@@ -268,26 +303,33 @@
     )(core_index, sums, keep, got)
 
     own = lax.all_to_all(outgoing, "dp", split_axis=0, concat_axis=0, tiled=True)
-    factor, keep, give, own = lax.optimization_barrier((factor, keep, give, own))
+    finished = orthogonalize(own.reshape(n_rows * half, columns))
+
+    finished, factor = lax.optimization_barrier((finished, factor))
+    back = lax.all_to_all(
+        finished.reshape(n_rows, half, columns), "dp", split_axis=0, concat_axis=0, tiled=True
+    )
     new_momentum = pl.pallas_call(
         momentum_kernel,
         out_shape=jax.ShapeDtypeStruct(momentum.shape, F32),
-        in_specs=[SMEM] + [VMEM] * 3,
+        in_specs=[VMEM] + [PINNED] * 2,
         out_specs=VMEM,
-        compiler_params=params(8),
+        scratch_shapes=[
+            pltpu.VMEM(grad.shape, grad.dtype),
+            pltpu.VMEM(momentum.shape, F32),
+            pltpu.SemaphoreType.DMA((2,)),
+        ],
+        compiler_params=params(10),
         name="momentum",
-    )(core_index, factor, keep, give)
-    own = own.reshape(n_rows * half, columns)
-    finished = orthogonalize(own, swap_cores(own))
-
-    finished, new_momentum = lax.optimization_barrier((finished, new_momentum))
-    back = lax.all_to_all(
-        finished.reshape(n_rows, half, columns), "dp", split_axis=0, concat_axis=0, tiled=True
+    )(factor, *inputs)
+    back, new_momentum = lax.optimization_barrier((back, new_momentum))
+
+    theirs = lax.dynamic_slice(
+        back, ((1 - core) * groups, 0, 0), (groups, half, columns), allow_negative_indices=False
     )
-    theirs = lax.dynamic_slice_in_dim(back, (1 - core) * groups, groups, 0)
     got = swap_cores(theirs)
-    update = place(True, core_index, back, grad.shape)
-    update = place(False, core_index, got, grad.shape, (update,))
+    update = place_own(core_index, back, grad.shape)
+    update = place_got(core_index, got, update)
     return (new_momentum, update)
 
 

time: 140 us -> 139 us (level)
  waiting for transfers between devices: 39.1 us -> 36.4 us
  Pallas kernels: 19.7 us -> 21.3 us
    all_to_all x1, waiting for transfers between devices: 37.7 us -> 34.7 us  [body(): lax.all_to_all(finished.reshape(n_rows, half, columns), 'dp', split_axis=...]
    pallas_call x1, Pallas kernels: 1.38 us -> 3.06 us  [body(): pl.pallas_call(momentum_kernel, out_shape=jax.ShapeDtypeStruct(momentum.s...]
    pallas_call x3 -> x4, Pallas kernels: 3.07 us -> 3.83 us  [the longest x1 1.3 us: orthogonalize(): pl.pallas_call(gram_kernel, out_shape=(jax.ShapeDtypeStruct(square_, F32)...]
    ppermute x3 -> x4, starting transfers between devices: 8.98 us -> 9.35 us  [swap_cores(): return lax.ppermute(x, 'expert', [(i, i ^ 1) for i in range(n)])]
  transfers between devices with their start and end apart: 4 -> 5, of which waited for: 3 -> 4; matrix products, arithmetic and copies ran while one was open for 0% -> 0% of each run, Pallas kernels for 3% -> 4%
where the time goes in v3:
time: 139 us
  blocking collectives  66.3 us (48%)
  waiting for transfers between devices  36.4 us (26%)
  Pallas kernels  21.3 us (15%)
  starting transfers between devices  13.7 us (10%)
    all_to_all x1, blocking collectives, body(): lax.all_to_all(outgoing, 'dp', split_axis=0, concat_axis=0, tiled=True)  41 us
    all_to_all x1, waiting for transfers between devices, body(): lax.all_to_all(finished.reshape(n_rows, half, columns), 'dp', split_axis=...  34.7 us
    all_to_all x1, blocking collectives, body(): lax.all_to_all(tile, ('dp', 'expert'), split_axis=0, concat_axis=0, tiled...  25.3 us
    pallas_call x1, Pallas kernels, orthogonalize(): pl.pallas_call(poly_kernel, out_shape=jax.ShapeDtypeStruct(wide, F32), in...  12.3 us
    ppermute x4, starting transfers between devices, swap_cores(): return lax.ppermute(x, 'expert', [(i, i ^ 1) for i in range(n)])  9.35 us
    all_to_all x1, starting transfers between devices, body(): lax.all_to_all(finished.reshape(n_rows, half, columns), 'dp', split_axis=...  4.35 us
    pallas_call x1, Pallas kernels, body(): pl.pallas_call(momentum_kernel, out_shape=jax.ShapeDtypeStruct(momentum.s...  3.06 us
  transfers between devices with their start and end apart: 5, of which 4 were waited for; matrix products, arithmetic and copies ran while one was open for 0% of the time, Pallas kernels for 4%

profile of v3, /device:TPU:1, one launch (start us, length us, event | category | flops | bytes accessed | tf_op | source)
XLA Modules:
  0.0 138.7 jit_solution(1121134465850529953)
XLA Ops:
  0.6 1.6 %prepare.1 = (f32[256,1,128]{2,1,0:T(1,128)S(1)}, f32[2,16,16,768]{3,2,1,0:T(8,128)S(1)}, f32[2,16,16,768]{3,2,1,0:T(8,128)S(1)}) custom-call(s32[1]{0:T(128)} %bitcast.core_ref.refs_0_, bf16[16,32,768]{2,1,0:T(8,128)(2,1)} %grad_ref.3, f32[16,32,768]{2,1,0:T(8,128)} %momentum_ref.3), custom_call_target="tpu_custom_call" | custom-call | tf_op jit(solution)/shard_map/prepare/pallas_call | solution.py:282
  2.3 3.3 %collective-permute-start = (f32[2,16,16,768]{3,2,1,0:T(8,128)S(1)}, f32[2,16,16,768]{3,2,1,0:T(8,128)S(1)}, u32[]{:S(2)}, u32[]{:S(2)}) collective-permute-start(f32[2,16,16,768]{3,2,1,0:T(8,128)S(1)} %get-tuple-element.16), channel_id=1, source_target_pairs={{0,1},{1,0},{2,3},{3,2},{4,5},{5,4},{6,7},{7,6},{8,9},{9,8},{10,11... | collective-permute-start | bytes 4718600 | tf_op jit(solution)/shard_map/ppermute | solution.py:33
  5.6 25.3 %all_to_all.15.refs_1_ = f32[256,1,128]{2,1,0:T(1,128)S(1)} all-to-all(f32[256,1,128]{2,1,0:T(1,128)S(1)} %get-tuple-element.14), channel_id=1, replica_groups=mesh['dp'=32,'expert'=8] {'dp','expert'}, dimensions={0} | all-to-all | bytes 262144 | tf_op jit(solution)/shard_map/all_to_all | solution.py:291
  30.9 0.0 collective-permute-done.refs_3_
  30.9 0.5 mix.1
  31.4 41.0 %all_to_all.16 = f32[32,16,768]{2,1,0:T(8,128)S(1)} all-to-all(f32[32,16,768]{2,1,0:T(8,128)S(1)} %get-tuple-element.17), channel_id=1, replica_groups=mesh['dp'=32,'expert'=8] {'dp'}, dimensions={0} | all-to-all | bytes 3145728 | tf_op jit(solution)/shard_map/all_to_all | solution.py:305
  72.4 0.1 fusion
  72.5 3.3 %collective-permute-start.1 = (f32[256,768]{1,0:T(8,128)S(1)}, f32[256,768]{1,0:T(8,128)S(1)}, u32[]{:S(2)}, u32[]{:S(2)}) collective-permute-start(f32[256,768]{1,0:T(8,128)S(1)} %bitcast.7), channel_id=1, source_target_pairs={{0,1},{1,0},{2,3},{3,2},{4,5},{5,4},{6,7},{7,6},{8,9},{9,8},{10,11... | collective-permute-start | bytes 2359304 | tf_op jit(solution)/shard_map/ppermute | solution.py:33
  75.8 0.3 collective-permute-start.2
  76.1 1.3 gram.1
  77.4 0.3 collective-permute-done.1.x_ref
  77.8 0.8 more_gram.1.part_ref
  78.5 0.4 collective-permute-done.2.other_ref
  78.9 12.3 %poly.1 = f32[512,768]{1,0:T(8,128)} custom-call(bf16[512,768]{1,0:T(8,128)(2,1)S(1)} %get-tuple-element.18.xh, bf16[512,768]{1,0:T(8,128)(2,1)S(1)} %get-tuple-element.19.xl, f32[768,768]{1,0:T(8,128)S(1)} %more_gram.1.part_ref, f32[256,768]{1,0:T(8,128)S(1)} %collective-permute-done.2.other_ref), custom_call_target="tpu_custom_call" | custom-call | tf_op jit(solution)/shard_map/poly/pallas_call | solution.py:257
  91.2 4.4 %all-to-all-start.2 = ((f32[32,16,768]{2,1,0:T(8,128)}), f32[32,16,768]{2,1,0:T(8,128)S(1)}, u32[]{:S(2)}, u32[]{:S(2)}) async-start(f32[32,16,768]{2,1,0:T(8,128)} %bitcast.4), calls=%async_computation.2 | async-start | bytes 3145728 | tf_op jit(solution)/shard_map/all_to_all | solution.py:309
  95.5 3.1 %momentum.1 = f32[16,32,768]{2,1,0:T(8,128)} custom-call(f32[8,128]{1,0:T(8,128)S(1)} %get-tuple-element.23.factor_ref, bf16[16,32,768]{2,1,0:T(8,128)(2,1)} %grad_ref.3, f32[16,32,768]{2,1,0:T(8,128)} %momentum_ref.3), custom_call_target="tpu_custom_call" | custom-call | tf_op jit(solution)/shard_map/momentum/pallas_call | solution.py:312
  98.6 34.7 %all-to-all-done.2.values_ref = f32[32,16,768]{2,1,0:T(8,128)S(1)} async-done(((f32[32,16,768]{2,1,0:T(8,128)}), f32[32,16,768]{2,1,0:T(8,128)S(1)}, u32[]{:S(2)}, u32[]{:S(2)}) %all-to-all-start.2) | async-done | bytes 1572896 | tf_op jit(solution)/shard_map/all_to_all | solution.py:309
  133.3 0.1 constant_dynamic-slice_fusion
  133.3 2.4 %collective-permute-start.3 = (f32[16,16,768]{2,1,0:T(8,128)S(1)}, f32[16,16,768]{2,1,0:T(8,128)S(1)}, u32[]{:S(2)}, u32[]{:S(2)}) collective-permute-start(f32[16,16,768]{2,1,0:T(8,128)S(1)} %constant_dynamic-slice_fusion), channel_id=1, source_target_pairs={{0,1},{1,0},{2,3},{3,2},{4,5},{5,4},{6,7},{7,6},{8,9},{9,8},{10,11... | collective-permute-start | bytes 2359304 | tf_op jit(solution)/shard_map/ppermute | solution.py:33
  135.7 0.9 place_own.1.before_ref
  136.6 1.0 collective-permute-done.3.values_ref
  137.6 0.9 place_got.1
Async XLA Ops:
  2.3 28.7 %collective-permute-start = (f32[2,16,16,768]{3,2,1,0:T(8,128)S(1)}, f32[2,16,16,768]{3,2,1,0:T(8,128)S(1)}, u32[]{:S(2)}, u32[]{:S(2)}) collective-permute-start(f32[2,16,16,768]{3,2,1,0:T(8,128)S(1)} %get-tuple-element.16), channel_id=1, source_target_pairs={{0,1},{1,0},{2,3},{3,2},{4,5},{5,4},{6,7},{7,6},{8,9},{9,8},{10,11... | collective-permute-start | bytes 4718600 | tf_op jit(solution)/shard_map/ppermute | solution.py:33
  72.5 5.3 %collective-permute-start.1 = (f32[256,768]{1,0:T(8,128)S(1)}, f32[256,768]{1,0:T(8,128)S(1)}, u32[]{:S(2)}, u32[]{:S(2)}) collective-permute-start(f32[256,768]{1,0:T(8,128)S(1)} %bitcast.7), channel_id=1, source_target_pairs={{0,1},{1,0},{2,3},{3,2},{4,5},{5,4},{6,7},{7,6},{8,9},{9,8},{10,11... | collective-permute-start | bytes 2359304 | tf_op jit(solution)/shard_map/ppermute | solution.py:33
  75.8 3.0 %collective-permute-start.2 = (f32[256,768]{1,0:T(8,128)S(1)}, f32[256,768]{1,0:T(8,128)S(1)}, u32[]{:S(2)}, u32[]{:S(2)}) collective-permute-start(f32[256,768]{1,0:T(8,128)S(1)} %bitcast.6), channel_id=1, source_target_pairs={{0,1},{1,0},{2,3},{3,2},{4,5},{5,4},{6,7},{7,6},{8,9},{9,8},{10,11... | collective-permute-start | bytes 2359304 | tf_op jit(solution)/shard_map/ppermute | solution.py:33
  91.2 42.1 %all-to-all-start.2 = ((f32[32,16,768]{2,1,0:T(8,128)}), f32[32,16,768]{2,1,0:T(8,128)S(1)}, u32[]{:S(2)}, u32[]{:S(2)}) async-start(f32[32,16,768]{2,1,0:T(8,128)} %bitcast.4), calls=%async_computation.2 | async-start | bytes 3145728 | tf_op jit(solution)/shard_map/all_to_all | solution.py:309
  133.3 4.3 %collective-permute-start.3 = (f32[16,16,768]{2,1,0:T(8,128)S(1)}, f32[16,16,768]{2,1,0:T(8,128)S(1)}, u32[]{:S(2)}, u32[]{:S(2)}) collective-permute-start(f32[16,16,768]{2,1,0:T(8,128)S(1)} %constant_dynamic-slice_fusion), channel_id=1, source_target_pairs={{0,1},{1,0},{2,3},{3,2},{4,5},{5,4},{6,7},{7,6},{8,9},{9,8},{10,11... | collective-permute-start | bytes 2359304 | tf_op jit(solution)/shard_map/ppermute | solution.py:33

commit v4 on v3

--- a/solution.py
+++ b/solution.py
@@ -12,6 +12,7 @@
 ITERS = 2
 BLOCK = 256
 NB = C // BLOCK
+Y = 4
 PAIRS = [(i, j) for i in range(NB) for j in range(i, NB)]
 
 A0, A1, A2 = 3.4445, -4.775, 2.0315
@@ -31,6 +32,15 @@
 def swap_cores(x):
     n = lax.axis_size("expert")
     return lax.ppermute(x, "expert", [(i, i ^ 1) for i in range(n)])
+
+
+def exchange_rows(x):
+    z_size = lax.axis_size("dp") // Y
+    fold = [z for k in range(z_size // 2) for z in (k, z_size - 1 - k)]
+    group = [z * Y + y for y in range(Y) for z in fold]
+    return lax.all_to_all(
+        x, "dp", split_axis=0, concat_axis=0, tiled=True, axis_index_groups=[group]
+    )
 
 
 def split(v):
@@ -185,7 +195,9 @@
         g_ref[blk(i), blk(j)] = before_ref[blk(i), blk(j)] + square(th, tl, xh, xl, i, j)
 
 
-def poly_kernel(xh, xl, part_ref, other_ref, out_ref, raw, yh, yl, th, tl, gh, gl, mh, ml, nh, nl):
+def poly_kernel(
+    xh, xl, part_ref, other_ref, out_ref, raw, yh, yl, th, tl, gh, gl, mh, ml, nh, nl, stage, sems
+):
     some = pl.ds(0, other_ref.shape[0])
     oh, ol = yh.at[some], yl.at[some]
     split_both_ways(other_ref, oh, ol, th, tl)
@@ -222,9 +234,15 @@
         put_symmetric(mh, ml, i, j, v)
     polynomial(mh, ml, nh, nl, A1, A2)
     scale = 0.2 * math.sqrt(max(R, C))
+    copies = []
     for i in rows:
         for j in range(NB):
-            out_ref[blk(i), blk(j)] = scale * dot3(yh[blk(i), :], yl[blk(i), :], nh[:, blk(j)], nl[:, blk(j)])
+            place = (blk(i), blk(j))
+            stage[place] = scale * dot3(yh[blk(i), :], yl[blk(i), :], nh[:, blk(j)], nl[:, blk(j)])
+            copies.append(pltpu.make_async_copy(stage.at[place], out_ref.at[place], sems.at[len(copies)]))
+            copies[-1].start()
+    for copy in copies:
+        copy.wait()
 
 
 def orthogonalize(own):
@@ -258,11 +276,12 @@
         poly_kernel,
         out_shape=jax.ShapeDtypeStruct(wide, F32),
         in_specs=[VMEM] * 4,
-        out_specs=VMEM,
+        out_specs=HBM,
         scratch_shapes=[pltpu.VMEM(square_, F32)]
         + [pltpu.VMEM(wide, BF16)] * 2
         + split_scratch[2:]
-        + [pltpu.VMEM(square_, BF16)] * 6,
+        + [pltpu.VMEM(square_, BF16)] * 6
+        + [pltpu.VMEM(wide, F32), pltpu.SemaphoreType.DMA((n // BLOCK * NB,))],
         compiler_params=params(24),
         name="poly",
     )(xh, xl, part, last)
@@ -302,13 +321,11 @@
         name="mix",
     )(core_index, sums, keep, got)
 
-    own = lax.all_to_all(outgoing, "dp", split_axis=0, concat_axis=0, tiled=True)
+    own = exchange_rows(outgoing)
     finished = orthogonalize(own.reshape(n_rows * half, columns))
 
     finished, factor = lax.optimization_barrier((finished, factor))
-    back = lax.all_to_all(
-        finished.reshape(n_rows, half, columns), "dp", split_axis=0, concat_axis=0, tiled=True
-    )
+    back = exchange_rows(finished.reshape(n_rows, half, columns))
     new_momentum = pl.pallas_call(
         momentum_kernel,
         out_shape=jax.ShapeDtypeStruct(momentum.shape, F32),

time: 139 us -> 138 us (level)
  waiting for transfers between devices: 36.4 us -> 34.1 us
    all_to_all x1, waiting for transfers between devices: 34.7 us -> 32.4 us  [exchange_rows(): lax.all_to_all(x, 'dp', split_axis=0, concat_axis=0, tiled=True, axis_ind...]
where the time goes in v4:
time: 138 us; the launch traced here: 136 us
  blocking collectives  65.8 us (48%)
  waiting for transfers between devices  34.1 us (25%)
  Pallas kernels  20.9 us (15%)
  starting transfers between devices  14.7 us (11%)
    all_to_all x1, blocking collectives, exchange_rows(): lax.all_to_all(x, 'dp', split_axis=0, concat_axis=0, tiled=True, axis_ind...  40.5 us
    all_to_all x1, waiting for transfers between devices, exchange_rows(): lax.all_to_all(x, 'dp', split_axis=0, concat_axis=0, tiled=True, axis_ind...  32.4 us
    all_to_all x1, blocking collectives, body(): lax.all_to_all(tile, ('dp', 'expert'), split_axis=0, concat_axis=0, tiled...  25.3 us
    pallas_call x1, Pallas kernels, orthogonalize(): pl.pallas_call(poly_kernel, out_shape=jax.ShapeDtypeStruct(wide, F32), in...  11.8 us
    ppermute x4, starting transfers between devices, swap_cores(): return lax.ppermute(x, 'expert', [(i, i ^ 1) for i in range(n)])  8.96 us
    all_to_all x1, starting transfers between devices, exchange_rows(): lax.all_to_all(x, 'dp', split_axis=0, concat_axis=0, tiled=True, axis_ind...  5.7 us
    pallas_call x1, Pallas kernels, body(): pl.pallas_call(momentum_kernel, out_shape=jax.ShapeDtypeStruct(momentum.s...  3.06 us
  transfers between devices with their start and end apart: 5, of which 4 were waited for; matrix products, arithmetic and copies ran while one was open for 0% of the time, Pallas kernels for 4%

profile of v4, /device:TPU:1, one launch (start us, length us, event | category | flops | bytes accessed | tf_op | source)
XLA Modules:
  0.0 136.4 jit_solution(8453203498393868266)
XLA Ops:
  0.6 1.6 %prepare.1 = (f32[256,1,128]{2,1,0:T(1,128)S(1)}, f32[2,16,16,768]{3,2,1,0:T(8,128)S(1)}, f32[2,16,16,768]{3,2,1,0:T(8,128)S(1)}) custom-call(s32[1]{0:T(128)} %bitcast.core_ref.refs_0_, bf16[16,32,768]{2,1,0:T(8,128)(2,1)} %grad_ref.3, f32[16,32,768]{2,1,0:T(8,128)} %momentum_ref.3), custom_call_target="tpu_custom_call" | custom-call | tf_op jit(solution)/shard_map/prepare/pallas_call | solution.py:301
  2.3 3.3 %collective-permute-start = (f32[2,16,16,768]{3,2,1,0:T(8,128)S(1)}, f32[2,16,16,768]{3,2,1,0:T(8,128)S(1)}, u32[]{:S(2)}, u32[]{:S(2)}) collective-permute-start(f32[2,16,16,768]{3,2,1,0:T(8,128)S(1)} %get-tuple-element.16), channel_id=1, source_target_pairs={{0,1},{1,0},{2,3},{3,2},{4,5},{5,4},{6,7},{7,6},{8,9},{9,8},{10,11... | collective-permute-start | bytes 4718600 | tf_op jit(solution)/shard_map/ppermute | solution.py:34
  5.6 25.3 %all_to_all.15.refs_1_ = f32[256,1,128]{2,1,0:T(1,128)S(1)} all-to-all(f32[256,1,128]{2,1,0:T(1,128)S(1)} %get-tuple-element.14), channel_id=1, replica_groups=mesh['dp'=32,'expert'=8] {'dp','expert'}, dimensions={0} | all-to-all | bytes 262144 | tf_op jit(solution)/shard_map/all_to_all | solution.py:310
  30.9 0.0 collective-permute-done.refs_3_
  30.9 0.5 mix.1
  31.4 40.5 %all_to_all.16 = f32[32,16,768]{2,1,0:T(8,128)S(1)} all-to-all(f32[32,16,768]{2,1,0:T(8,128)S(1)} %get-tuple-element.17), channel_id=1, replica_groups={{0,224,32,192,64,160,96,128,8,232,40,200,72,168,104,136,16,240,48,208,8..., dimensions={0} | all-to-all | bytes 3145728 | tf_op jit(solution)/shard_map/all_to_all | solution.py:41
  71.9 0.1 fusion
  72.0 2.5 %collective-permute-start.1 = (f32[256,768]{1,0:T(8,128)S(1)}, f32[256,768]{1,0:T(8,128)S(1)}, u32[]{:S(2)}, u32[]{:S(2)}) collective-permute-start(f32[256,768]{1,0:T(8,128)S(1)} %bitcast.7), channel_id=1, source_target_pairs={{0,1},{1,0},{2,3},{3,2},{4,5},{5,4},{6,7},{7,6},{8,9},{9,8},{10,11... | collective-permute-start | bytes 2359304 | tf_op jit(solution)/shard_map/ppermute | solution.py:34
  74.6 0.3 collective-permute-start.2
  74.9 1.3 gram.1
  76.2 0.3 collective-permute-done.1.x_ref
  76.5 0.8 more_gram.1.part_ref
  77.3 0.4 collective-permute-done.2.other_ref
  77.6 11.8 %poly.1 = f32[512,768]{1,0:T(8,128)} custom-call(bf16[512,768]{1,0:T(8,128)(2,1)S(1)} %get-tuple-element.18.xh, bf16[512,768]{1,0:T(8,128)(2,1)S(1)} %get-tuple-element.19.xl, f32[768,768]{1,0:T(8,128)S(1)} %more_gram.1.part_ref, f32[256,768]{1,0:T(8,128)S(1)} %collective-permute-done.2.other_ref), custom_call_target="tpu_custom_call" | custom-call | tf_op jit(solution)/shard_map/poly/pallas_call | solution.py:275
  89.5 5.7 %all-to-all-start.2 = ((f32[32,16,768]{2,1,0:T(8,128)}), f32[32,16,768]{2,1,0:T(8,128)S(1)}, u32[]{:S(2)}, u32[]{:S(2)}) async-start(f32[32,16,768]{2,1,0:T(8,128)} %bitcast.4), calls=%async_computation.2 | async-start | bytes 3145728 | tf_op jit(solution)/shard_map/all_to_all | solution.py:41
  95.2 3.1 %momentum.1 = f32[16,32,768]{2,1,0:T(8,128)} custom-call(f32[8,128]{1,0:T(8,128)S(1)} %get-tuple-element.23.factor_ref, bf16[16,32,768]{2,1,0:T(8,128)(2,1)} %grad_ref.3, f32[16,32,768]{2,1,0:T(8,128)} %momentum_ref.3), custom_call_target="tpu_custom_call" | custom-call | tf_op jit(solution)/shard_map/momentum/pallas_call | solution.py:329
  98.2 32.4 %all-to-all-done.2.values_ref = f32[32,16,768]{2,1,0:T(8,128)S(1)} async-done(((f32[32,16,768]{2,1,0:T(8,128)}), f32[32,16,768]{2,1,0:T(8,128)S(1)}, u32[]{:S(2)}, u32[]{:S(2)}) %all-to-all-start.2) | async-done | bytes 1572896 | tf_op jit(solution)/shard_map/all_to_all | solution.py:41
  130.6 0.1 constant_dynamic-slice_fusion
  130.7 2.8 %collective-permute-start.3 = (f32[16,16,768]{2,1,0:T(8,128)S(1)}, f32[16,16,768]{2,1,0:T(8,128)S(1)}, u32[]{:S(2)}, u32[]{:S(2)}) collective-permute-start(f32[16,16,768]{2,1,0:T(8,128)S(1)} %constant_dynamic-slice_fusion), channel_id=1, source_target_pairs={{0,1},{1,0},{2,3},{3,2},{4,5},{5,4},{6,7},{7,6},{8,9},{9,8},{10,11... | collective-permute-start | bytes 2359304 | tf_op jit(solution)/shard_map/ppermute | solution.py:34
  133.5 0.9 place_own.1.before_ref
  134.4 1.0 collective-permute-done.3.values_ref
  135.4 0.9 place_got.1
Async XLA Ops:
  2.3 28.7 %collective-permute-start = (f32[2,16,16,768]{3,2,1,0:T(8,128)S(1)}, f32[2,16,16,768]{3,2,1,0:T(8,128)S(1)}, u32[]{:S(2)}, u32[]{:S(2)}) collective-permute-start(f32[2,16,16,768]{3,2,1,0:T(8,128)S(1)} %get-tuple-element.16), channel_id=1, source_target_pairs={{0,1},{1,0},{2,3},{3,2},{4,5},{5,4},{6,7},{7,6},{8,9},{9,8},{10,11... | collective-permute-start | bytes 4718600 | tf_op jit(solution)/shard_map/ppermute | solution.py:34
  72.0 4.5 %collective-permute-start.1 = (f32[256,768]{1,0:T(8,128)S(1)}, f32[256,768]{1,0:T(8,128)S(1)}, u32[]{:S(2)}, u32[]{:S(2)}) collective-permute-start(f32[256,768]{1,0:T(8,128)S(1)} %bitcast.7), channel_id=1, source_target_pairs={{0,1},{1,0},{2,3},{3,2},{4,5},{5,4},{6,7},{7,6},{8,9},{9,8},{10,11... | collective-permute-start | bytes 2359304 | tf_op jit(solution)/shard_map/ppermute | solution.py:34
  74.6 3.0 %collective-permute-start.2 = (f32[256,768]{1,0:T(8,128)S(1)}, f32[256,768]{1,0:T(8,128)S(1)}, u32[]{:S(2)}, u32[]{:S(2)}) collective-permute-start(f32[256,768]{1,0:T(8,128)S(1)} %bitcast.6), channel_id=1, source_target_pairs={{0,1},{1,0},{2,3},{3,2},{4,5},{5,4},{6,7},{7,6},{8,9},{9,8},{10,11... | collective-permute-start | bytes 2359304 | tf_op jit(solution)/shard_map/ppermute | solution.py:34
  89.5 41.1 %all-to-all-start.2 = ((f32[32,16,768]{2,1,0:T(8,128)}), f32[32,16,768]{2,1,0:T(8,128)S(1)}, u32[]{:S(2)}, u32[]{:S(2)}) async-start(f32[32,16,768]{2,1,0:T(8,128)} %bitcast.4), calls=%async_computation.2 | async-start | bytes 3145728 | tf_op jit(solution)/shard_map/all_to_all | solution.py:41
  130.7 4.7 %collective-permute-start.3 = (f32[16,16,768]{2,1,0:T(8,128)S(1)}, f32[16,16,768]{2,1,0:T(8,128)S(1)}, u32[]{:S(2)}, u32[]{:S(2)}) collective-permute-start(f32[16,16,768]{2,1,0:T(8,128)S(1)} %constant_dynamic-slice_fusion), channel_id=1, source_target_pairs={{0,1},{1,0},{2,3},{3,2},{4,5},{5,4},{6,7},{7,6},{8,9},{9,8},{10,11... | collective-permute-start | bytes 2359304 | tf_op jit(solution)/shard_map/ppermute | solution.py:34
